TPU v7x, 512 devices: a whole 4x4x16 slice. The times are simulated.
512 devices in a mesh: pm: 2 (over y_lo), ka: 128 (over x, z, core), isdf: 2 (over y_hi).
Axes of the slice: x: 4, y: 4 (y_hi: 2, y_lo: 2; y = y_hi * 2 + y_lo), z: 16, core: 2. Of those that a mesh axis runs over, the one named last changes fastest.
Arguments:
- amplitudes: bfloat16 [2, 2, 2, 256, 64, 256], P('pm', None, None, 'ka'), may hold values from -6 to 6
- conduction: bfloat16 [2, 256, 256, 512], P(None, 'ka', None, 'isdf'), may hold values from -0.375 to 0.375
- valence: bfloat16 [2, 256, 64, 512], P(None, 'ka'), may hold values from -0.75 to 0.75
- energy: float32 [256, 64, 256], P('ka', None, 'isdf'), may hold values from 0.5 to 2.5
- screened: bfloat16 [4, 2, 512, 512], P(None, None, 'isdf'), may hold values from -0.59765625 to 0.59765625
- coulomb: float32 [512, 512], P(None, 'isdf'), may hold values from -0.03125 to 0.03125
- mirror: int32 [256], P('ka'), may hold values from 0 to 255, as said below
- transfer_class: int32 [256, 256], P('ka'), may hold values from 0 to 3, as said below
Outputs:
- response: bfloat16 [2, 2, 2, 256, 64, 256], P('pm', None, None, 'ka', None, 'isdf')
Inputs may be any that keep to these rules, and one draw needn't show every extreme that they name: mirror[mirror[k]] = k; a k-point of block j (the aligned block of 2 k-points that holds it) has its mirror in block 127 - j. transfer_class[k, k2] depends only on (k - k2) mod 256.
All inputs are finite; a program needn't handle non-finite values.
Results may differ from a plain program's by a relative error of at most 0.015.
Values may be sent and summed in bfloat16 or wider, within the bound.
A program may use at most 128 MiB of HBM per device.

v0:
```python
import jax
import jax.numpy as jnp
from jax import lax
from jax.sharding import PartitionSpec as P

REACH = 2
HIGHEST = lax.Precision.HIGHEST


def swapped(block, axis, apart):
    count = lax.axis_size(axis)
    route = []
    for low in range(count):
        high = low | 1 << apart
        if high != low and high < count:
            route += [(low, high), (high, low)]
    return lax.ppermute(block, axis, route)


def shifted(value, axis, by):
    size = lax.axis_size(axis)
    return lax.ppermute(value, axis, [(i, (i + by) % size) for i in range(size)])


def pair_einsum(pattern, left, right, conjugate):

    def single(first, second):
        return jnp.einsum(pattern, first, second, preferred_element_type=jnp.float32)

    if conjugate:
        real_part = single(left[0], right[0]) + single(left[1], right[1])
        imag_part = single(left[1], right[0]) - single(left[0], right[1])
    else:
        real_part = single(left[0], right[0]) - single(left[1], right[1])
        imag_part = single(left[0], right[1]) + single(left[1], right[0])
    return (real_part, imag_part)


def conjugated(field):
    return jnp.stack([field[:, 0], -field[:, 1]], axis=1)


def coefficients(vector, conduction):
    real_part, imag_part = pair_einsum(
        "bkvc,kcm->bkvm", (vector[:, 0], vector[:, 1]), (conduction[0], conduction[1]), False
    )
    return jnp.stack([real_part, imag_part], axis=1).astype(jnp.bfloat16)


def amp_bits(field):
    for bit_number in range(lax.axis_size("ka").bit_length() - 1):
        field = swapped(field, "ka", bit_number)
    return field


def result_bits(field):
    for bit_number in range(lax.axis_size("ka").bit_length() - 1):
        field = swapped(field, "ka", bit_number)
    return field


def by_mirror(field, local_mirror):
    index = local_mirror[None, None, :, None, None]
    return jnp.where(index == 0, field[:, :, 0:1], field[:, :, 1:2])


def per_device(amplitudes, conduction, valence, energy, screened, coulomb, mirror, transfer_class):
    pm_index = lax.axis_index("pm")
    ka_index = lax.axis_index("ka")
    isdf_index = lax.axis_index("isdf")
    ka_count = lax.axis_size("ka")
    kpoint_count = conduction.shape[1]
    mu_count = conduction.shape[3]
    point_count = valence.shape[3]
    cond_share = energy.shape[2]
    vector_count = amplitudes.shape[1]
    is_plus = pm_index == 0
    parity = jnp.where(is_plus, 1.0, -1.0).astype(jnp.float32)
    exchange_weight = jnp.where(is_plus, 4.0, 0.0).astype(jnp.float32)
    local_amps = amplitudes[0]
    partner_amps = swapped(local_amps, "pm", 0)
    partner_side = jnp.where(is_plus, partner_amps, local_amps)
    distant_side = amp_bits(partner_side)
    direct = jnp.where(is_plus, local_amps, partner_amps).astype(jnp.float32)
    local_mirror = mirror - (ka_count - 1 - ka_index) * kpoint_count
    flipped = conjugated(by_mirror(distant_side, local_mirror).astype(jnp.float32))
    vector = (direct + parity * flipped).astype(jnp.bfloat16)
    own_coef = coefficients(vector, conduction)
    valence_part = lax.dynamic_slice_in_dim(valence, isdf_index * mu_count, mu_count, 3)
    rho_real = jnp.einsum(
        "kvm,bkvm->bm", valence_part[0], own_coef[:, 0], preferred_element_type=jnp.float32
    )
    rho_real = rho_real + jnp.einsum(
        "kvm,bkvm->bm", valence_part[1], own_coef[:, 1], preferred_element_type=jnp.float32
    )
    rho_imag = jnp.einsum(
        "kvm,bkvm->bm", valence_part[0], own_coef[:, 1], preferred_element_type=jnp.float32
    )
    rho_imag = rho_imag - jnp.einsum(
        "kvm,bkvm->bm", valence_part[1], own_coef[:, 0], preferred_element_type=jnp.float32
    )
    density = jnp.stack([rho_real, rho_imag], axis=1)
    spread = jnp.einsum("nm,brm->brn", coulomb, density, precision=HIGHEST)
    spread = lax.psum(spread, ("ka", "isdf"))
    potential = lax.dynamic_slice_in_dim(spread, isdf_index * mu_count, mu_count, 2)
    class_ids = jnp.arange(screened.shape[0], dtype=jnp.int32)

    def accumulate(totals, coef_block, valence_block, source):
        pair_real, pair_imag = pair_einsum(
            "bqvm,qvn->bqmn",
            (coef_block[:, 0], coef_block[:, 1]),
            (valence_block[0], valence_block[1]),
            True,
        )
        pair_real = pair_real.astype(jnp.bfloat16)
        pair_imag = pair_imag.astype(jnp.bfloat16)
        classes = lax.dynamic_slice_in_dim(transfer_class, source * kpoint_count, kpoint_count, 1)
        selector = (classes[:, :, None] == class_ids).astype(jnp.bfloat16)
        total_real, total_imag = totals
        for visitor in range(kpoint_count):
            chosen = jnp.einsum(
                "kw,wrmn->rkmn", selector[:, visitor], screened, preferred_element_type=jnp.float32
            ).astype(jnp.bfloat16)
            screen_real = chosen[0][None].astype(jnp.float32)
            screen_imag = chosen[1][None].astype(jnp.float32)
            visit_real = pair_real[:, visitor][:, None].astype(jnp.float32)
            visit_imag = pair_imag[:, visitor][:, None].astype(jnp.float32)
            total_real = total_real + (screen_real * visit_real - screen_imag * visit_imag)
            total_imag = total_imag + (screen_real * visit_imag + screen_imag * visit_real)
        return (total_real, total_imag)

    payload = (vector, conduction, valence)

    def advance(moving, offset):
        return shifted((moving[0], moving[1], moving[2]), "ka", offset)

    def unpack(moving):
        return (coefficients(moving[0], moving[1]), moving[2])

    def visit(totals, moving, distance):
        coef_block, valence_block = unpack(moving)
        source = jnp.mod(ka_index + distance, ka_count)
        return accumulate(totals, coef_block, valence_block, source)

    zero_field = jnp.zeros((vector_count, kpoint_count, mu_count, point_count), jnp.float32)
    totals = accumulate((zero_field, zero_field), own_coef, valence, ka_index)
    below_item = payload
    for count_done in range(REACH):
        below_item = advance(below_item, 1)
        totals = visit(totals, below_item, -(count_done + 1))
    above_item = payload
    for count_done in range(REACH):
        above_item = advance(above_item, -1)
        totals = visit(totals, above_item, count_done + 1)
    sum_real = totals[0].astype(jnp.bfloat16)
    sum_imag = totals[1].astype(jnp.bfloat16)
    back_real, back_imag = pair_einsum(
        "bkmn,kvn->bkvm", (sum_real, sum_imag), (valence[0], valence[1]), False
    )
    potential_real = potential[:, 0][:, None, None, :]
    potential_imag = potential[:, 1][:, None, None, :]
    exchange_real = potential_real * valence_part[0] - potential_imag * valence_part[1]
    exchange_imag = potential_real * valence_part[1] + potential_imag * valence_part[0]
    field_real = (exchange_weight * exchange_real - back_real).astype(jnp.bfloat16)
    field_imag = (exchange_weight * exchange_imag - back_imag).astype(jnp.bfloat16)
    out_real, out_imag = pair_einsum(
        "bkvm,kcm->bkvc", (field_real, field_imag), (conduction[0], conduction[1]), True
    )
    partial_out = jnp.stack([out_real, out_imag], axis=1)
    summed = lax.psum_scatter(
        partial_out.astype(jnp.bfloat16), "isdf", scatter_dimension=4, tiled=True
    ).astype(jnp.float32)
    vector_part = lax.dynamic_slice_in_dim(vector, isdf_index * cond_share, cond_share, 4).astype(
        jnp.float32
    )
    channel_out = (energy[None, None] * vector_part + summed).astype(jnp.bfloat16)
    partner_out = swapped(channel_out, "pm", 0)
    blended = (
        0.5 * (partner_out.astype(jnp.float32) + parity * channel_out.astype(jnp.float32))
    ).astype(jnp.bfloat16)
    distant_out = result_bits(blended)
    reflected = conjugated(by_mirror(distant_out, local_mirror))
    result = jnp.where(is_plus, blended, reflected)
    return result[None]


def solution(mesh):
    return jax.shard_map(
        per_device,
        mesh=mesh,
        in_specs=(
            P("pm", None, None, "ka", None, None),
            P(None, "ka", None, "isdf"),
            P(None, "ka", None, None),
            P("ka", None, "isdf"),
            P(None, None, "isdf", None),
            P(None, "isdf"),
            P("ka"),
            P("ka", None),
        ),
        out_specs=P("pm", None, None, "ka", None, "isdf"),
        check_vma=False,
    )
```

profile of v0, /device:TPU:2, one launch (start us, length us, event | category | flops | bytes accessed | tf_op | source)
XLA Modules:
  0.0 1086.2 jit_solution(11353441118219177994)
XLA Ops:
  8.6 10.8 collective-permute-start.15
  21.3 5.8 collective-permute-start.16
  28.1 3.5 collective-permute-start
  32.8 3.2 copy.48
  59.1 3.0 fusion.87
  66.2 3.5 fusion.75
  78.0 6.5 collective-permute-done.2
  88.5 12.3 %collective-permute-done.3 = bf16[2,2,2,64,256]{4,3,0,2,1:T(8,128)(2,1)S(1)} collective-permute-done((bf16[2,2,2,64,256]{4,3,0,2,1:T(8,128)(2,1)S(1)}, bf16[2,2,2,64,256]{4,3,0,2,1:T(8,128)(2,1)S(1)}, u32[]{:S(2)}, u32[]{:S(2)}) %collective-permute-start.3) | collective-permute-done | bytes 262176 | tf_op jit(solution)/shard_map/ppermute | solution.py:17
  105.3 22.7 %collective-permute-done.4 = bf16[2,2,2,64,256]{4,3,0,2,1:T(8,128)(2,1)S(1)} collective-permute-done((bf16[2,2,2,64,256]{4,3,0,2,1:T(8,128)(2,1)S(1)}, bf16[2,2,2,64,256]{4,3,0,2,1:T(8,128)(2,1)S(1)}, u32[]{:S(2)}, u32[]{:S(2)}) %collective-permute-start.4) | collective-permute-done | bytes 262176 | tf_op jit(solution)/shard_map/ppermute | solution.py:17
  128.0 14.7 %collective-permute-start.5 = (bf16[2,2,2,64,256]{4,3,0,2,1:T(8,128)(2,1)S(1)}, bf16[2,2,2,64,256]{4,3,0,2,1:T(8,128)(2,1)S(1)}, u32[]{:S(2)}, u32[]{:S(2)}) collective-permute-start(bf16[2,2,2,64,256]{4,3,0,2,1:T(8,128)(2,1)S(1)} %collective-permute-done.4), channel_id=1, source_target_pairs={{0,32},{32,0},{2,34},{34,2},{4,36},{36,4},{6,38},{38,6},{8,40},{40... | collective-permute-start | bytes 786440 | tf_op jit(solution)/shard_map/ppermute | solution.py:17
  144.7 14.9 %collective-permute-done.5 = bf16[2,2,2,64,256]{4,3,0,2,1:T(8,128)(2,1)S(1)} collective-permute-done((bf16[2,2,2,64,256]{4,3,0,2,1:T(8,128)(2,1)S(1)}, bf16[2,2,2,64,256]{4,3,0,2,1:T(8,128)(2,1)S(1)}, u32[]{:S(2)}, u32[]{:S(2)}) %collective-permute-start.5) | collective-permute-done | bytes 262176 | tf_op jit(solution)/shard_map/ppermute | solution.py:17
  164.4 5.4 collective-permute-done.6
  169.8 4.2 collective-permute-start.7
  200.1 5.8 collective-permute-start.19
  207.9 5.8 collective-permute-start.18
  225.0 583.0 %psum.7 = f32[2,2,512]{2,1,0:T(2,128)S(1)} all-reduce(f32[2,2,512]{2,1,0:T(2,128)S(1)} %fusion.90), channel_id=1, replica_groups=mesh['pm'=2,'ka'=128,'isdf'=2] {'ka','isdf'}, use_global_device_ids=true, to_apply=%region_0.1 | all-reduce | flops 2048 | bytes 16384 | tf_op jit(solution)/shard_map/psum | solution.py:104
  842.2 5.3 collective-permute-start.17
  875.2 9.2 add_convert_fusion
  884.5 9.5 add_convert_fusion.1
  898.4 92.4 %reduce-scatter.4.cloned.1.call-done = bf16[128,512]{1,0:T(8,128)(2,1)} async-done(((bf16[256,512]{1,0:T(8,128)(2,1)}), bf16[128,512]{1,0:T(8,128)(2,1)}) %reduce-scatter.4.cloned.1.call-update) | async-done | bytes 131088
  995.6 4.6 collective-permute-done.20
  1003.5 3.5 collective-permute-start.22
  1007.0 4.0 collective-permute-done.22
  1011.0 4.4 collective-permute-start.23
  1015.4 5.9 collective-permute-done.23
  1021.3 7.6 collective-permute-start.24
  1028.9 9.8 collective-permute-done.24
  1038.7 12.0 %collective-permute-start.25 = (bf16[2,2,2,64,128]{4,3,0,2,1:T(8,128)(2,1)S(1)}, bf16[2,2,2,64,128]{4,3,0,2,1:T(8,128)(2,1)S(1)}, u32[]{:S(2)}, u32[]{:S(2)}) collective-permute-start(bf16[2,2,2,64,128]{4,3,0,2,1:T(8,128)(2,1)S(1)} %collective-permute-done.24), channel_id=1, source_target_pairs={{0,32},{32,0},{2,34},{34,2},{4,36},{36,4},{6,38},{38,6},{8,40},{40... | collective-permute-start | bytes 393224 | tf_op jit(solution)/shard_map/ppermute | solution.py:17
  1050.8 12.1 %collective-permute-done.25 = bf16[2,2,2,64,128]{4,3,0,2,1:T(8,128)(2,1)S(1)} collective-permute-done((bf16[2,2,2,64,128]{4,3,0,2,1:T(8,128)(2,1)S(1)}, bf16[2,2,2,64,128]{4,3,0,2,1:T(8,128)(2,1)S(1)}, u32[]{:S(2)}, u32[]{:S(2)}) %collective-permute-start.25) | collective-permute-done | bytes 131104 | tf_op jit(solution)/shard_map/ppermute | solution.py:17
  1065.3 4.4 collective-permute-done.26
  1069.7 4.0 collective-permute-start.27
  1073.7 4.4 collective-permute-done.27
  (284 shorter events, 172.9 us)
Async XLA Ops:
  6.5 218.0 %copy-start = (f32[512,256]{1,0:T(8,128)S(1)}, f32[512,256]{1,0:T(8,128)}, u32[]{:S(2)}) copy-start(f32[512,256]{1,0:T(8,128)} %param.13) | copy-start | bytes 1572868
  6.5 984.3 %reduce-scatter.4.cloned.1.call-start = ((), (), s32[]{:S(2)}) async-start(), calls=%async_computation.1 | async-start | bytes 393216
  6.5 199.4 %collective-permute-start.9 = (bf16[2,2,256,256]{3,2,1,0:T(8,128)(2,1)}, bf16[2,2,256,256]{3,2,1,0:T(8,128)(2,1)}, u32[]{:S(2)}, u32[]{:S(2)}) collective-permute-start(bf16[2,2,256,256]{3,2,1,0:T(8,128)(2,1)} %param.9), channel_id=1, source_target_pairs={{0,2},{2,4},{4,6},{6,8},{8,10},{10,12},{12,14},{14,16},{16,18},{18... | collective-permute-start | bytes 1572872 | tf_op jit(solution)/shard_map/ppermute | solution.py:22
  8.6 199.3 %collective-permute-start.15 = (bf16[2,2,256,256]{3,2,1,0:T(8,128)(2,1)}, bf16[2,2,256,256]{3,2,1,0:T(8,128)(2,1)}, u32[]{:S(2)}, u32[]{:S(2)}) collective-permute-start(bf16[2,2,256,256]{3,2,1,0:T(8,128)(2,1)} %param.9), channel_id=1, source_target_pairs={{0,254},{2,0},{4,2},{6,4},{8,6},{10,8},{12,10},{14,12},{16,14},{18... | collective-permute-start | bytes 1572872 | tf_op jit(solution)/shard_map/ppermute | solution.py:22
  19.4 178.6 %collective-permute-start.10 = (bf16[2,2,64,512]{3,2,1,0:T(8,128)(2,1)}, bf16[2,2,64,512]{3,2,1,0:T(8,128)(2,1)}, u32[]{:S(2)}, u32[]{:S(2)}) collective-permute-start(bf16[2,2,64,512]{3,2,1,0:T(8,128)(2,1)} %param.10), channel_id=1, source_target_pairs={{0,2},{2,4},{4,6},{6,8},{8,10},{10,12},{12,14},{14,16},{16,18},{18... | collective-permute-start | bytes 786440 | tf_op jit(solution)/shard_map/ppermute | solution.py:22
  21.3 178.8 %collective-permute-start.16 = (bf16[2,2,64,512]{3,2,1,0:T(8,128)(2,1)}, bf16[2,2,64,512]{3,2,1,0:T(8,128)(2,1)}, u32[]{:S(2)}, u32[]{:S(2)}) collective-permute-start(bf16[2,2,64,512]{3,2,1,0:T(8,128)(2,1)} %param.10), channel_id=1, source_target_pairs={{0,254},{2,0},{4,2},{6,4},{8,6},{10,8},{12,10},{14,12},{16,14},{18... | collective-permute-start | bytes 786440 | tf_op jit(solution)/shard_map/ppermute | solution.py:22
  28.1 41.6 %collective-permute-start = (bf16[2,2,2,64,256]{4,3,0,2,1:T(8,128)(2,1)S(1)}, bf16[2,2,2,64,256]{4,3,0,2,1:T(8,128)(2,1)S(1)}, u32[]{:S(2)}, u32[]{:S(2)}) collective-permute-start(bf16[2,2,2,64,256]{4,3,0,2,1:T(8,128)(2,1)S(1)} %bitcast.655), channel_id=1, source_target_pairs={{0,256},{256,0},{1,257},{257,1},{2,258},{258,2},{3,259},{259,3},{4... | collective-permute-start | bytes 786440 | tf_op jit(solution)/shard_map/ppermute | solution.py:17
  69.7 4.1 collective-permute-start.1
  73.9 10.7 collective-permute-start.2
  84.6 16.3 %collective-permute-start.3 = (bf16[2,2,2,64,256]{4,3,0,2,1:T(8,128)(2,1)S(1)}, bf16[2,2,2,64,256]{4,3,0,2,1:T(8,128)(2,1)S(1)}, u32[]{:S(2)}, u32[]{:S(2)}) collective-permute-start(bf16[2,2,2,64,256]{4,3,0,2,1:T(8,128)(2,1)S(1)} %collective-permute-done.2), channel_id=1, source_target_pairs={{0,8},{8,0},{2,10},{10,2},{4,12},{12,4},{6,14},{14,6},{16,24},{24,... | collective-permute-start | bytes 786440 | tf_op jit(solution)/shard_map/ppermute | solution.py:17
  100.8 27.1 %collective-permute-start.4 = (bf16[2,2,2,64,256]{4,3,0,2,1:T(8,128)(2,1)S(1)}, bf16[2,2,2,64,256]{4,3,0,2,1:T(8,128)(2,1)S(1)}, u32[]{:S(2)}, u32[]{:S(2)}) collective-permute-start(bf16[2,2,2,64,256]{4,3,0,2,1:T(8,128)(2,1)S(1)} %collective-permute-done.3), channel_id=1, source_target_pairs={{0,16},{16,0},{2,18},{18,2},{4,20},{20,4},{6,22},{22,6},{8,24},{24... | collective-permute-start | bytes 786440 | tf_op jit(solution)/shard_map/ppermute | solution.py:17
  128.0 31.6 %collective-permute-start.5 = (bf16[2,2,2,64,256]{4,3,0,2,1:T(8,128)(2,1)S(1)}, bf16[2,2,2,64,256]{4,3,0,2,1:T(8,128)(2,1)S(1)}, u32[]{:S(2)}, u32[]{:S(2)}) collective-permute-start(bf16[2,2,2,64,256]{4,3,0,2,1:T(8,128)(2,1)S(1)} %collective-permute-done.4), channel_id=1, source_target_pairs={{0,32},{32,0},{2,34},{34,2},{4,36},{36,4},{6,38},{38,6},{8,40},{40... | collective-permute-start | bytes 786440 | tf_op jit(solution)/shard_map/ppermute | solution.py:17
  159.6 10.2 collective-permute-start.6
  169.8 43.8 %collective-permute-start.7 = (bf16[2,2,2,64,256]{4,3,0,2,1:T(8,128)(2,1)}, bf16[2,2,2,64,256]{4,3,0,2,1:T(8,128)(2,1)}, u32[]{:S(2)}, u32[]{:S(2)}) collective-permute-start(bf16[2,2,2,64,256]{4,3,0,2,1:T(8,128)(2,1)} %collective-permute-done.6), channel_id=1, source_target_pairs={{0,128},{128,0},{2,130},{130,2},{4,132},{132,4},{6,134},{134,6},{8... | collective-permute-start | bytes 786440 | tf_op jit(solution)/shard_map/ppermute | solution.py:17
  198.1 654.0 %collective-permute-start.13 = (bf16[2,2,64,512]{3,2,1,0:T(8,128)(2,1)}, bf16[2,2,64,512]{3,2,1,0:T(8,128)(2,1)}, u32[]{:S(2)}, u32[]{:S(2)}) collective-permute-start(bf16[2,2,64,512]{3,2,1,0:T(8,128)(2,1)} %collective-permute-done.10), channel_id=1, source_target_pairs={{0,2},{2,4},{4,6},{6,8},{8,10},{10,12},{12,14},{14,16},{16,18},{18... | collective-permute-start | bytes 786440 | tf_op jit(solution)/shard_map/ppermute | solution.py:22
  200.1 664.4 %collective-permute-start.19 = (bf16[2,2,64,512]{3,2,1,0:T(8,128)(2,1)}, bf16[2,2,64,512]{3,2,1,0:T(8,128)(2,1)}, u32[]{:S(2)}, u32[]{:S(2)}) collective-permute-start(bf16[2,2,64,512]{3,2,1,0:T(8,128)(2,1)} %collective-permute-done.16), channel_id=1, source_target_pairs={{0,254},{2,0},{4,2},{6,4},{8,6},{10,8},{12,10},{14,12},{16,14},{18... | collective-permute-start | bytes 786440 | tf_op jit(solution)/shard_map/ppermute | solution.py:22
  205.9 636.3 %collective-permute-start.12 = (bf16[2,2,256,256]{3,2,1,0:T(8,128)(2,1)}, bf16[2,2,256,256]{3,2,1,0:T(8,128)(2,1)}, u32[]{:S(2)}, u32[]{:S(2)}) collective-permute-start(bf16[2,2,256,256]{3,2,1,0:T(8,128)(2,1)} %collective-permute-done.9), channel_id=1, source_target_pairs={{0,2},{2,4},{4,6},{6,8},{8,10},{10,12},{12,14},{14,16},{16,18},{18... | collective-permute-start | bytes 1572872 | tf_op jit(solution)/shard_map/ppermute | solution.py:22
  207.9 652.0 %collective-permute-start.18 = (bf16[2,2,256,256]{3,2,1,0:T(8,128)(2,1)}, bf16[2,2,256,256]{3,2,1,0:T(8,128)(2,1)}, u32[]{:S(2)}, u32[]{:S(2)}) collective-permute-start(bf16[2,2,256,256]{3,2,1,0:T(8,128)(2,1)} %collective-permute-done.15), channel_id=1, source_target_pairs={{0,254},{2,0},{4,2},{6,4},{8,6},{10,8},{12,10},{14,12},{16,14},{18... | collective-permute-start | bytes 1572872 | tf_op jit(solution)/shard_map/ppermute | solution.py:22
  217.9 594.7 %collective-permute-start.8 = (bf16[2,2,2,64,256]{4,3,0,2,1:T(8,128)(2,1)}, bf16[2,2,2,64,256]{4,3,0,2,1:T(8,128)(2,1)}, u32[]{:S(2)}, u32[]{:S(2)}) collective-permute-start(bf16[2,2,2,64,256]{4,3,0,2,1:T(8,128)(2,1)} %fusion.89), channel_id=1, source_target_pairs={{0,2},{2,4},{4,6},{6,8},{8,10},{10,12},{12,14},{14,16},{16,18},{18... | collective-permute-start | bytes 786440 | tf_op jit(solution)/shard_map/ppermute | solution.py:22
  225.0 584.7 %copy-start.46 = (bf16[2,2,64,256]{3,2,1,0:T(8,128)(2,1)S(1)}, bf16[2,2,64,256]{3,2,1,0:T(8,128)(2,1)}, u32[]{:S(2)}) copy-start(bf16[2,2,64,256]{3,2,1,0:T(8,128)(2,1)} %get-tuple-element.68) | copy-start | bytes 393220
  812.6 14.6 %collective-permute-start.14 = (bf16[2,2,2,64,256]{4,3,0,2,1:T(8,128)(2,1)}, bf16[2,2,2,64,256]{4,3,0,2,1:T(8,128)(2,1)S(1)}, u32[]{:S(2)}, u32[]{:S(2)}) collective-permute-start(bf16[2,2,2,64,256]{4,3,0,2,1:T(8,128)(2,1)} %fusion.89), channel_id=1, source_target_pairs={{0,254},{2,0},{4,2},{6,4},{8,6},{10,8},{12,10},{14,12},{16,14},{18... | collective-permute-start | bytes 786440 | tf_op jit(solution)/shard_map/ppermute | solution.py:22
  827.2 20.3 %collective-permute-start.11 = (bf16[2,2,2,64,256]{4,3,0,2,1:T(8,128)(2,1)}, bf16[2,2,2,64,256]{4,3,0,2,1:T(8,128)(2,1)S(1)}, u32[]{:S(2)}, u32[]{:S(2)}) collective-permute-start(bf16[2,2,2,64,256]{4,3,0,2,1:T(8,128)(2,1)} %collective-permute-done.8), channel_id=1, source_target_pairs={{0,2},{2,4},{4,6},{6,8},{8,10},{10,12},{12,14},{14,16},{16,18},{18... | collective-permute-start | bytes 786440 | tf_op jit(solution)/shard_map/ppermute | solution.py:22
  842.2 17.7 %collective-permute-start.17 = (bf16[2,2,2,64,256]{4,3,0,2,1:T(8,128)(2,1)S(1)}, bf16[2,2,2,64,256]{4,3,0,2,1:T(8,128)(2,1)S(1)}, u32[]{:S(2)}, u32[]{:S(2)}) collective-permute-start(bf16[2,2,2,64,256]{4,3,0,2,1:T(8,128)(2,1)S(1)} %collective-permute-done.14), channel_id=1, source_target_pairs={{0,254},{2,0},{4,2},{6,4},{8,6},{10,8},{12,10},{14,12},{16,14},{18... | collective-permute-start | bytes 786440 | tf_op jit(solution)/shard_map/ppermute | solution.py:22
  896.9 182.0 %copy-start.1 = (f32[512,256]{1,0:T(8,128)S(1)}, f32[512,256]{1,0:T(8,128)}, u32[]{:S(2)}) copy-start(f32[512,256]{1,0:T(8,128)} %param.13) | copy-start | bytes 1572868
  993.1 7.1 collective-permute-start.20
  1000.3 3.2 collective-permute-start.21
  1003.5 7.4 collective-permute-start.22
  1011.0 10.3 collective-permute-start.23
  1021.3 17.5 %collective-permute-start.24 = (bf16[2,2,2,64,128]{4,3,0,2,1:T(8,128)(2,1)S(1)}, bf16[2,2,2,64,128]{4,3,0,2,1:T(8,128)(2,1)S(1)}, u32[]{:S(2)}, u32[]{:S(2)}) collective-permute-start(bf16[2,2,2,64,128]{4,3,0,2,1:T(8,128)(2,1)S(1)} %collective-permute-done.23), channel_id=1, source_target_pairs={{0,16},{16,0},{2,18},{18,2},{4,20},{20,4},{6,22},{22,6},{8,24},{24... | collective-permute-start | bytes 393224 | tf_op jit(solution)/shard_map/ppermute | solution.py:17
  1038.7 24.1 %collective-permute-start.25 = (bf16[2,2,2,64,128]{4,3,0,2,1:T(8,128)(2,1)S(1)}, bf16[2,2,2,64,128]{4,3,0,2,1:T(8,128)(2,1)S(1)}, u32[]{:S(2)}, u32[]{:S(2)}) collective-permute-start(bf16[2,2,2,64,128]{4,3,0,2,1:T(8,128)(2,1)S(1)} %collective-permute-done.24), channel_id=1, source_target_pairs={{0,32},{32,0},{2,34},{34,2},{4,36},{36,4},{6,38},{38,6},{8,40},{40... | collective-permute-start | bytes 393224 | tf_op jit(solution)/shard_map/ppermute | solution.py:17
  1062.9 6.8 collective-permute-start.26
  1069.7 8.4 collective-permute-start.27
  (58 other events, 577.1 us)
Sparse Core Ops, SparseCore 0:
  898.5 92.2 reduce-scatter.3
where the time goes:
time: 1100 us; the launch traced here: 1090 us
  blocking collectives  583 us (53%)
  waiting for transfers between devices  201 us (18%)
  starting transfers between devices  120 us (11%)
  matrix products  76.3 us (7%)
  other arithmetic  56 us (5%)
  local copies, waits for them, and re-layouts  35.4 us (3%)
  between operations  15.1 us (1%)
    psum x1, blocking collectives, per_device(): spread = lax.psum(spread, ('ka', 'isdf'))  583 us
    ppermute x16, waiting for transfers between devices, swapped(): return lax.ppermute(block, axis, route)  108 us
    unnamed x2, waiting for transfers between devices  92.5 us
    ppermute x16, starting transfers between devices, swapped(): return lax.ppermute(block, axis, route)  71.9 us
    dot_general x48, matrix products, single(): jnp.einsum(pattern, first, second, preferred_element_type=jnp.float32)  53.4 us
    ppermute x12, starting transfers between devices, shifted(): lax.ppermute(value, axis, [(i, (i + by) % size) for i in range(size)])  47.7 us
    mul x10, other arithmetic, accumulate(): screen_real * visit_real - screen_imag * visit_imag  23 us
    dot_general x10, matrix products, accumulate(): jnp.einsum('kw,wrmn->rkmn', selector[:, visitor], screened, preferred_ele...  22.4 us
  transfers between devices with their start and end apart: 29, of which 14 were waited for; matrix products, arithmetic and copies ran while one was open for 12% of the time, Pallas kernels for 0%

commit v1 on v0

--- a/solution.py
+++ b/solution.py
@@ -101,7 +101,7 @@
     )
     density = jnp.stack([rho_real, rho_imag], axis=1)
     spread = jnp.einsum("nm,brm->brn", coulomb, density, precision=HIGHEST)
-    spread = lax.psum(spread, ("ka", "isdf"))
+    spread = lax.psum(lax.psum(spread, "ka"), "isdf")
     potential = lax.dynamic_slice_in_dim(spread, isdf_index * mu_count, mu_count, 2)
     class_ids = jnp.arange(screened.shape[0], dtype=jnp.int32)
 

time: 1100 us -> 700 us (0.64)
  the two profiles are of different devices: /device:TPU:2 before, /device:TPU:4 now
where the time goes in v1:
time: 700 us; the launch traced here: 690 us
  blocking collectives  223 us (32%)
  waiting for transfers between devices  167 us (24%)
  starting transfers between devices  118 us (17%)
  matrix products  76.2 us (11%)
  other arithmetic  55.9 us (8%)
  local copies, waits for them, and re-layouts  35.3 us (5%)
  between operations  15.1 us (2%)
    psum x2, blocking collectives, per_device(): spread = lax.psum(lax.psum(spread, 'ka'), 'isdf')  223 us
    ppermute x16, waiting for transfers between devices, swapped(): return lax.ppermute(block, axis, route)  109 us
    ppermute x16, starting transfers between devices, swapped(): return lax.ppermute(block, axis, route)  69.9 us
    unnamed x2, waiting for transfers between devices  57.9 us
    dot_general x48, matrix products, single(): jnp.einsum(pattern, first, second, preferred_element_type=jnp.float32)  53.4 us
    ppermute x12, starting transfers between devices, shifted(): lax.ppermute(value, axis, [(i, (i + by) % size) for i in range(size)])  47.7 us
    mul x10, other arithmetic, accumulate(): screen_real * visit_real - screen_imag * visit_imag  22.9 us
    dot_general x10, matrix products, accumulate(): jnp.einsum('kw,wrmn->rkmn', selector[:, visitor], screened, preferred_ele...  22.4 us
  transfers between devices with their start and end apart: 29, of which 14 were waited for; matrix products, arithmetic and copies ran while one was open for 19% of the time, Pallas kernels for 0%

profile of v1, /device:TPU:4, one launch (start us, length us, event | category | flops | bytes accessed | tf_op | source)
XLA Modules:
  0.0 689.6 jit_solution(9333920358687279829)
XLA Ops:
  8.6 10.8 %collective-permute-start.15 = (bf16[2,2,256,256]{3,2,1,0:T(8,128)(2,1)}, bf16[2,2,256,256]{3,2,1,0:T(8,128)(2,1)}, u32[]{:S(2)}, u32[]{:S(2)}) collective-permute-start(bf16[2,2,256,256]{3,2,1,0:T(8,128)(2,1)} %param.9), channel_id=1, source_target_pairs={{0,254},{2,0},{4,2},{6,4},{8,6},{10,8},{12,10},{14,12},{16,14},{18... | collective-permute-start | bytes 1572872 | tf_op jit(solution)/shard_map/ppermute | solution.py:22
  21.3 5.8 collective-permute-start.16
  28.1 3.5 collective-permute-start
  32.7 3.2 copy.48
  59.0 3.0 fusion.87
  66.1 3.5 fusion.75
  77.9 6.5 collective-permute-done.2
  88.5 12.3 %collective-permute-done.3 = bf16[2,2,2,64,256]{4,3,0,2,1:T(8,128)(2,1)S(1)} collective-permute-done((bf16[2,2,2,64,256]{4,3,0,2,1:T(8,128)(2,1)S(1)}, bf16[2,2,2,64,256]{4,3,0,2,1:T(8,128)(2,1)S(1)}, u32[]{:S(2)}, u32[]{:S(2)}) %collective-permute-start.3) | collective-permute-done | bytes 262176 | tf_op jit(solution)/shard_map/ppermute | solution.py:17
  105.3 22.6 %collective-permute-done.4 = bf16[2,2,2,64,256]{4,3,0,2,1:T(8,128)(2,1)S(1)} collective-permute-done((bf16[2,2,2,64,256]{4,3,0,2,1:T(8,128)(2,1)S(1)}, bf16[2,2,2,64,256]{4,3,0,2,1:T(8,128)(2,1)S(1)}, u32[]{:S(2)}, u32[]{:S(2)}) %collective-permute-start.4) | collective-permute-done | bytes 262176 | tf_op jit(solution)/shard_map/ppermute | solution.py:17
  127.9 14.7 %collective-permute-start.5 = (bf16[2,2,2,64,256]{4,3,0,2,1:T(8,128)(2,1)S(1)}, bf16[2,2,2,64,256]{4,3,0,2,1:T(8,128)(2,1)S(1)}, u32[]{:S(2)}, u32[]{:S(2)}) collective-permute-start(bf16[2,2,2,64,256]{4,3,0,2,1:T(8,128)(2,1)S(1)} %collective-permute-done.4), channel_id=1, source_target_pairs={{0,32},{32,0},{2,34},{34,2},{4,36},{36,4},{6,38},{38,6},{8,40},{40... | collective-permute-start | bytes 786440 | tf_op jit(solution)/shard_map/ppermute | solution.py:17
  144.7 14.9 %collective-permute-done.5 = bf16[2,2,2,64,256]{4,3,0,2,1:T(8,128)(2,1)S(1)} collective-permute-done((bf16[2,2,2,64,256]{4,3,0,2,1:T(8,128)(2,1)S(1)}, bf16[2,2,2,64,256]{4,3,0,2,1:T(8,128)(2,1)S(1)}, u32[]{:S(2)}, u32[]{:S(2)}) %collective-permute-start.5) | collective-permute-done | bytes 262176 | tf_op jit(solution)/shard_map/ppermute | solution.py:17
  159.6 3.1 collective-permute-start.6
  164.7 5.0 collective-permute-done.6
  198.6 5.8 collective-permute-start.19
  206.4 5.8 collective-permute-start.18
  223.5 216.0 %psum.14 = f32[2,2,512]{2,1,0:T(2,128)S(1)} all-reduce(f32[2,2,512]{2,1,0:T(2,128)S(1)} %fusion.90), channel_id=1, replica_groups=mesh['pm'=2,'ka'=128,'isdf'=2] {'ka'}, use_global_device_ids=true, to_apply=%region_0.1 | all-reduce | flops 2048 | bytes 16384 | tf_op jit(solution)/shard_map/psum | solution.py:104
  439.5 6.5 psum.15
  480.2 5.3 collective-permute-start.17
  513.2 9.2 %add_convert_fusion = bf16[2,2,256,512]{3,2,0,1:T(8,128)(2,1)S(1)} fusion(f32[2,256,512]{2,1,0:T(8,128)} %get-tuple-element.46, f32[2,256,512]{2,1,0:T(8,128)S(1)} %copy-done.19, f32[2,256,512]{2,1,0:T(8,128)} %get-tuple-element.71, f32[2,256,512]{2,1,0:T(8,128)S(1)} %copy-done.18, f32[2,256,512]{2,1,0:T(8,128)} %get-tuple-element.45, ...), kind=kLoop, calls=%fused_computation | loop fusion | flops 20971520 | bytes 42991616 | tf_op jit(solution)/shard_map/convert_element_type | solution.py:156
  522.4 9.5 %add_convert_fusion.1 = bf16[2,2,256,512]{3,2,0,1:T(8,128)(2,1)S(1)} fusion(f32[2,256,512]{2,1,0:T(8,128)} %get-tuple-element.46, f32[2,256,512]{2,1,0:T(8,128)S(1)} %copy-done.19, f32[2,256,512]{2,1,0:T(8,128)} %get-tuple-element.71, f32[2,256,512]{2,1,0:T(8,128)S(1)} %copy-done.18, f32[2,256,512]{2,1,0:T(8,128)} %get-tuple-element.45, ...), kind=kLoop, calls=%fused_computation.1 | loop fusion | flops 20971520 | bytes 42991616 | tf_op jit(solution)/shard_map/convert_element_type | solution.py:155
  536.3 57.9 %reduce-scatter.4.cloned.1.call-done = bf16[128,512]{1,0:T(8,128)(2,1)} async-done(((bf16[256,512]{1,0:T(8,128)(2,1)}), bf16[128,512]{1,0:T(8,128)(2,1)}) %reduce-scatter.4.cloned.1.call-update) | async-done | bytes 131088
  599.0 4.6 collective-permute-done.20
  606.9 3.5 collective-permute-start.22
  610.4 4.0 collective-permute-done.22
  614.4 4.4 collective-permute-start.23
  618.8 5.9 collective-permute-done.23
  624.7 7.7 %collective-permute-start.24 = (bf16[2,2,2,64,128]{4,3,0,2,1:T(8,128)(2,1)S(1)}, bf16[2,2,2,64,128]{4,3,0,2,1:T(8,128)(2,1)S(1)}, u32[]{:S(2)}, u32[]{:S(2)}) collective-permute-start(bf16[2,2,2,64,128]{4,3,0,2,1:T(8,128)(2,1)S(1)} %collective-permute-done.23), channel_id=1, source_target_pairs={{0,16},{16,0},{2,18},{18,2},{4,20},{20,4},{6,22},{22,6},{8,24},{24... | collective-permute-start | bytes 393224 | tf_op jit(solution)/shard_map/ppermute | solution.py:17
  632.3 9.9 %collective-permute-done.24 = bf16[2,2,2,64,128]{4,3,0,2,1:T(8,128)(2,1)S(1)} collective-permute-done((bf16[2,2,2,64,128]{4,3,0,2,1:T(8,128)(2,1)S(1)}, bf16[2,2,2,64,128]{4,3,0,2,1:T(8,128)(2,1)S(1)}, u32[]{:S(2)}, u32[]{:S(2)}) %collective-permute-start.24) | collective-permute-done | bytes 131104 | tf_op jit(solution)/shard_map/ppermute | solution.py:17
  642.2 12.0 %collective-permute-start.25 = (bf16[2,2,2,64,128]{4,3,0,2,1:T(8,128)(2,1)S(1)}, bf16[2,2,2,64,128]{4,3,0,2,1:T(8,128)(2,1)S(1)}, u32[]{:S(2)}, u32[]{:S(2)}) collective-permute-start(bf16[2,2,2,64,128]{4,3,0,2,1:T(8,128)(2,1)S(1)} %collective-permute-done.24), channel_id=1, source_target_pairs={{0,32},{32,0},{2,34},{34,2},{4,36},{36,4},{6,38},{38,6},{8,40},{40... | collective-permute-start | bytes 393224 | tf_op jit(solution)/shard_map/ppermute | solution.py:17
  654.2 12.1 %collective-permute-done.25 = bf16[2,2,2,64,128]{4,3,0,2,1:T(8,128)(2,1)S(1)} collective-permute-done((bf16[2,2,2,64,128]{4,3,0,2,1:T(8,128)(2,1)S(1)}, bf16[2,2,2,64,128]{4,3,0,2,1:T(8,128)(2,1)S(1)}, u32[]{:S(2)}, u32[]{:S(2)}) %collective-permute-start.25) | collective-permute-done | bytes 131104 | tf_op jit(solution)/shard_map/ppermute | solution.py:17
  669.3 3.9 collective-permute-done.26
  675.5 6.0 collective-permute-done.27
  (285 shorter events, 175.7 us)
Async XLA Ops:
  6.5 216.4 %copy-start = (f32[512,256]{1,0:T(8,128)S(1)}, f32[512,256]{1,0:T(8,128)}, u32[]{:S(2)}) copy-start(f32[512,256]{1,0:T(8,128)} %param.13) | copy-start | bytes 1572868
  6.5 587.7 %reduce-scatter.4.cloned.1.call-start = ((), (), s32[]{:S(2)}) async-start(), calls=%async_computation.1 | async-start | bytes 393216
  6.5 197.9 %collective-permute-start.9 = (bf16[2,2,256,256]{3,2,1,0:T(8,128)(2,1)}, bf16[2,2,256,256]{3,2,1,0:T(8,128)(2,1)}, u32[]{:S(2)}, u32[]{:S(2)}) collective-permute-start(bf16[2,2,256,256]{3,2,1,0:T(8,128)(2,1)} %param.9), channel_id=1, source_target_pairs={{0,2},{2,4},{4,6},{6,8},{8,10},{10,12},{12,14},{14,16},{16,18},{18... | collective-permute-start | bytes 1572872 | tf_op jit(solution)/shard_map/ppermute | solution.py:22
  8.6 197.8 %collective-permute-start.15 = (bf16[2,2,256,256]{3,2,1,0:T(8,128)(2,1)}, bf16[2,2,256,256]{3,2,1,0:T(8,128)(2,1)}, u32[]{:S(2)}, u32[]{:S(2)}) collective-permute-start(bf16[2,2,256,256]{3,2,1,0:T(8,128)(2,1)} %param.9), channel_id=1, source_target_pairs={{0,254},{2,0},{4,2},{6,4},{8,6},{10,8},{12,10},{14,12},{16,14},{18... | collective-permute-start | bytes 1572872 | tf_op jit(solution)/shard_map/ppermute | solution.py:22
  19.4 177.1 %collective-permute-start.10 = (bf16[2,2,64,512]{3,2,1,0:T(8,128)(2,1)}, bf16[2,2,64,512]{3,2,1,0:T(8,128)(2,1)}, u32[]{:S(2)}, u32[]{:S(2)}) collective-permute-start(bf16[2,2,64,512]{3,2,1,0:T(8,128)(2,1)} %param.10), channel_id=1, source_target_pairs={{0,2},{2,4},{4,6},{6,8},{8,10},{10,12},{12,14},{14,16},{16,18},{18... | collective-permute-start | bytes 786440 | tf_op jit(solution)/shard_map/ppermute | solution.py:22
  21.3 177.3 %collective-permute-start.16 = (bf16[2,2,64,512]{3,2,1,0:T(8,128)(2,1)}, bf16[2,2,64,512]{3,2,1,0:T(8,128)(2,1)}, u32[]{:S(2)}, u32[]{:S(2)}) collective-permute-start(bf16[2,2,64,512]{3,2,1,0:T(8,128)(2,1)} %param.10), channel_id=1, source_target_pairs={{0,254},{2,0},{4,2},{6,4},{8,6},{10,8},{12,10},{14,12},{16,14},{18... | collective-permute-start | bytes 786440 | tf_op jit(solution)/shard_map/ppermute | solution.py:22
  28.1 41.5 %collective-permute-start = (bf16[2,2,2,64,256]{4,3,0,2,1:T(8,128)(2,1)S(1)}, bf16[2,2,2,64,256]{4,3,0,2,1:T(8,128)(2,1)S(1)}, u32[]{:S(2)}, u32[]{:S(2)}) collective-permute-start(bf16[2,2,2,64,256]{4,3,0,2,1:T(8,128)(2,1)S(1)} %bitcast.655), channel_id=1, source_target_pairs={{0,256},{256,0},{1,257},{257,1},{2,258},{258,2},{3,259},{259,3},{4... | collective-permute-start | bytes 786440 | tf_op jit(solution)/shard_map/ppermute | solution.py:17
  69.7 4.1 collective-permute-start.1
  73.8 10.7 %collective-permute-start.2 = (bf16[2,2,2,64,256]{4,3,0,2,1:T(8,128)(2,1)S(1)}, bf16[2,2,2,64,256]{4,3,0,2,1:T(8,128)(2,1)S(1)}, u32[]{:S(2)}, u32[]{:S(2)}) collective-permute-start(bf16[2,2,2,64,256]{4,3,0,2,1:T(8,128)(2,1)S(1)} %collective-permute-done.1), channel_id=1, source_target_pairs={{0,4},{4,0},{2,6},{6,2},{8,12},{12,8},{10,14},{14,10},{16,20},{20,... | collective-permute-start | bytes 786440 | tf_op jit(solution)/shard_map/ppermute | solution.py:17
  84.5 16.3 %collective-permute-start.3 = (bf16[2,2,2,64,256]{4,3,0,2,1:T(8,128)(2,1)S(1)}, bf16[2,2,2,64,256]{4,3,0,2,1:T(8,128)(2,1)S(1)}, u32[]{:S(2)}, u32[]{:S(2)}) collective-permute-start(bf16[2,2,2,64,256]{4,3,0,2,1:T(8,128)(2,1)S(1)} %collective-permute-done.2), channel_id=1, source_target_pairs={{0,8},{8,0},{2,10},{10,2},{4,12},{12,4},{6,14},{14,6},{16,24},{24,... | collective-permute-start | bytes 786440 | tf_op jit(solution)/shard_map/ppermute | solution.py:17
  100.7 27.1 %collective-permute-start.4 = (bf16[2,2,2,64,256]{4,3,0,2,1:T(8,128)(2,1)S(1)}, bf16[2,2,2,64,256]{4,3,0,2,1:T(8,128)(2,1)S(1)}, u32[]{:S(2)}, u32[]{:S(2)}) collective-permute-start(bf16[2,2,2,64,256]{4,3,0,2,1:T(8,128)(2,1)S(1)} %collective-permute-done.3), channel_id=1, source_target_pairs={{0,16},{16,0},{2,18},{18,2},{4,20},{20,4},{6,22},{22,6},{8,24},{24... | collective-permute-start | bytes 786440 | tf_op jit(solution)/shard_map/ppermute | solution.py:17
  127.9 31.7 %collective-permute-start.5 = (bf16[2,2,2,64,256]{4,3,0,2,1:T(8,128)(2,1)S(1)}, bf16[2,2,2,64,256]{4,3,0,2,1:T(8,128)(2,1)S(1)}, u32[]{:S(2)}, u32[]{:S(2)}) collective-permute-start(bf16[2,2,2,64,256]{4,3,0,2,1:T(8,128)(2,1)S(1)} %collective-permute-done.4), channel_id=1, source_target_pairs={{0,32},{32,0},{2,34},{34,2},{4,36},{36,4},{6,38},{38,6},{8,40},{40... | collective-permute-start | bytes 786440 | tf_op jit(solution)/shard_map/ppermute | solution.py:17
  159.6 10.2 %collective-permute-start.6 = (bf16[2,2,2,64,256]{4,3,0,2,1:T(8,128)(2,1)S(1)}, bf16[2,2,2,64,256]{4,3,0,2,1:T(8,128)(2,1)}, u32[]{:S(2)}, u32[]{:S(2)}) collective-permute-start(bf16[2,2,2,64,256]{4,3,0,2,1:T(8,128)(2,1)S(1)} %collective-permute-done.5), channel_id=1, source_target_pairs={{0,64},{64,0},{2,66},{66,2},{4,68},{68,4},{6,70},{70,6},{8,72},{72... | collective-permute-start | bytes 786440 | tf_op jit(solution)/shard_map/ppermute | solution.py:17
  169.8 42.4 %collective-permute-start.7 = (bf16[2,2,2,64,256]{4,3,0,2,1:T(8,128)(2,1)}, bf16[2,2,2,64,256]{4,3,0,2,1:T(8,128)(2,1)}, u32[]{:S(2)}, u32[]{:S(2)}) collective-permute-start(bf16[2,2,2,64,256]{4,3,0,2,1:T(8,128)(2,1)} %collective-permute-done.6), channel_id=1, source_target_pairs={{0,128},{128,0},{2,130},{130,2},{4,132},{132,4},{6,134},{134,6},{8... | collective-permute-start | bytes 786440 | tf_op jit(solution)/shard_map/ppermute | solution.py:17
  196.6 293.5 %collective-permute-start.13 = (bf16[2,2,64,512]{3,2,1,0:T(8,128)(2,1)}, bf16[2,2,64,512]{3,2,1,0:T(8,128)(2,1)}, u32[]{:S(2)}, u32[]{:S(2)}) collective-permute-start(bf16[2,2,64,512]{3,2,1,0:T(8,128)(2,1)} %collective-permute-done.10), channel_id=1, source_target_pairs={{0,2},{2,4},{4,6},{6,8},{8,10},{10,12},{12,14},{14,16},{16,18},{18... | collective-permute-start | bytes 786440 | tf_op jit(solution)/shard_map/ppermute | solution.py:22
  198.6 303.9 %collective-permute-start.19 = (bf16[2,2,64,512]{3,2,1,0:T(8,128)(2,1)}, bf16[2,2,64,512]{3,2,1,0:T(8,128)(2,1)}, u32[]{:S(2)}, u32[]{:S(2)}) collective-permute-start(bf16[2,2,64,512]{3,2,1,0:T(8,128)(2,1)} %collective-permute-done.16), channel_id=1, source_target_pairs={{0,254},{2,0},{4,2},{6,4},{8,6},{10,8},{12,10},{14,12},{16,14},{18... | collective-permute-start | bytes 786440 | tf_op jit(solution)/shard_map/ppermute | solution.py:22
  204.4 275.8 %collective-permute-start.12 = (bf16[2,2,256,256]{3,2,1,0:T(8,128)(2,1)}, bf16[2,2,256,256]{3,2,1,0:T(8,128)(2,1)}, u32[]{:S(2)}, u32[]{:S(2)}) collective-permute-start(bf16[2,2,256,256]{3,2,1,0:T(8,128)(2,1)} %collective-permute-done.9), channel_id=1, source_target_pairs={{0,2},{2,4},{4,6},{6,8},{8,10},{10,12},{12,14},{14,16},{16,18},{18... | collective-permute-start | bytes 1572872 | tf_op jit(solution)/shard_map/ppermute | solution.py:22
  206.4 291.5 %collective-permute-start.18 = (bf16[2,2,256,256]{3,2,1,0:T(8,128)(2,1)}, bf16[2,2,256,256]{3,2,1,0:T(8,128)(2,1)}, u32[]{:S(2)}, u32[]{:S(2)}) collective-permute-start(bf16[2,2,256,256]{3,2,1,0:T(8,128)(2,1)} %collective-permute-done.15), channel_id=1, source_target_pairs={{0,254},{2,0},{4,2},{6,4},{8,6},{10,8},{12,10},{14,12},{16,14},{18... | collective-permute-start | bytes 1572872 | tf_op jit(solution)/shard_map/ppermute | solution.py:22
  216.3 234.2 %collective-permute-start.8 = (bf16[2,2,2,64,256]{4,3,0,2,1:T(8,128)(2,1)}, bf16[2,2,2,64,256]{4,3,0,2,1:T(8,128)(2,1)}, u32[]{:S(2)}, u32[]{:S(2)}) collective-permute-start(bf16[2,2,2,64,256]{4,3,0,2,1:T(8,128)(2,1)} %fusion.89), channel_id=1, source_target_pairs={{0,2},{2,4},{4,6},{6,8},{8,10},{10,12},{12,14},{14,16},{16,18},{18... | collective-permute-start | bytes 786440 | tf_op jit(solution)/shard_map/ppermute | solution.py:22
  223.5 224.2 %copy-start.46 = (bf16[2,2,64,256]{3,2,1,0:T(8,128)(2,1)S(1)}, bf16[2,2,64,256]{3,2,1,0:T(8,128)(2,1)}, u32[]{:S(2)}) copy-start(bf16[2,2,64,256]{3,2,1,0:T(8,128)(2,1)} %get-tuple-element.68) | copy-start | bytes 393220
  450.5 14.6 %collective-permute-start.14 = (bf16[2,2,2,64,256]{4,3,0,2,1:T(8,128)(2,1)}, bf16[2,2,2,64,256]{4,3,0,2,1:T(8,128)(2,1)S(1)}, u32[]{:S(2)}, u32[]{:S(2)}) collective-permute-start(bf16[2,2,2,64,256]{4,3,0,2,1:T(8,128)(2,1)} %fusion.89), channel_id=1, source_target_pairs={{0,254},{2,0},{4,2},{6,4},{8,6},{10,8},{12,10},{14,12},{16,14},{18... | collective-permute-start | bytes 786440 | tf_op jit(solution)/shard_map/ppermute | solution.py:22
  465.1 20.3 %collective-permute-start.11 = (bf16[2,2,2,64,256]{4,3,0,2,1:T(8,128)(2,1)}, bf16[2,2,2,64,256]{4,3,0,2,1:T(8,128)(2,1)S(1)}, u32[]{:S(2)}, u32[]{:S(2)}) collective-permute-start(bf16[2,2,2,64,256]{4,3,0,2,1:T(8,128)(2,1)} %collective-permute-done.8), channel_id=1, source_target_pairs={{0,2},{2,4},{4,6},{6,8},{8,10},{10,12},{12,14},{14,16},{16,18},{18... | collective-permute-start | bytes 786440 | tf_op jit(solution)/shard_map/ppermute | solution.py:22
  480.2 17.6 %collective-permute-start.17 = (bf16[2,2,2,64,256]{4,3,0,2,1:T(8,128)(2,1)S(1)}, bf16[2,2,2,64,256]{4,3,0,2,1:T(8,128)(2,1)S(1)}, u32[]{:S(2)}, u32[]{:S(2)}) collective-permute-start(bf16[2,2,2,64,256]{4,3,0,2,1:T(8,128)(2,1)S(1)} %collective-permute-done.14), channel_id=1, source_target_pairs={{0,254},{2,0},{4,2},{6,4},{8,6},{10,8},{12,10},{14,12},{16,14},{18... | collective-permute-start | bytes 786440 | tf_op jit(solution)/shard_map/ppermute | solution.py:22
  534.8 147.5 %copy-start.1 = (f32[512,256]{1,0:T(8,128)S(1)}, f32[512,256]{1,0:T(8,128)}, u32[]{:S(2)}) copy-start(f32[512,256]{1,0:T(8,128)} %param.13) | copy-start | bytes 1572868
  596.5 7.1 %collective-permute-start.20 = (bf16[2,2,2,64,128]{4,3,0,2,1:T(8,128)(2,1)S(1)}, bf16[2,2,2,64,128]{4,3,0,2,1:T(8,128)(2,1)S(1)}, u32[]{:S(2)}, u32[]{:S(2)}) collective-permute-start(bf16[2,2,2,64,128]{4,3,0,2,1:T(8,128)(2,1)S(1)} %add_convert_fusion.7), channel_id=1, source_target_pairs={{0,256},{256,0},{1,257},{257,1},{2,258},{258,2},{3,259},{259,3},{4... | collective-permute-start | bytes 393224 | tf_op jit(solution)/shard_map/ppermute | solution.py:17
  603.7 3.2 collective-permute-start.21
  606.9 7.4 %collective-permute-start.22 = (bf16[2,2,2,64,128]{4,3,0,2,1:T(8,128)(2,1)S(1)}, bf16[2,2,2,64,128]{4,3,0,2,1:T(8,128)(2,1)S(1)}, u32[]{:S(2)}, u32[]{:S(2)}) collective-permute-start(bf16[2,2,2,64,128]{4,3,0,2,1:T(8,128)(2,1)S(1)} %collective-permute-done.21), channel_id=1, source_target_pairs={{0,4},{4,0},{2,6},{6,2},{8,12},{12,8},{10,14},{14,10},{16,20},{20,... | collective-permute-start | bytes 393224 | tf_op jit(solution)/shard_map/ppermute | solution.py:17
  614.4 10.3 %collective-permute-start.23 = (bf16[2,2,2,64,128]{4,3,0,2,1:T(8,128)(2,1)S(1)}, bf16[2,2,2,64,128]{4,3,0,2,1:T(8,128)(2,1)S(1)}, u32[]{:S(2)}, u32[]{:S(2)}) collective-permute-start(bf16[2,2,2,64,128]{4,3,0,2,1:T(8,128)(2,1)S(1)} %collective-permute-done.22), channel_id=1, source_target_pairs={{0,8},{8,0},{2,10},{10,2},{4,12},{12,4},{6,14},{14,6},{16,24},{24,... | collective-permute-start | bytes 393224 | tf_op jit(solution)/shard_map/ppermute | solution.py:17
  624.7 17.5 %collective-permute-start.24 = (bf16[2,2,2,64,128]{4,3,0,2,1:T(8,128)(2,1)S(1)}, bf16[2,2,2,64,128]{4,3,0,2,1:T(8,128)(2,1)S(1)}, u32[]{:S(2)}, u32[]{:S(2)}) collective-permute-start(bf16[2,2,2,64,128]{4,3,0,2,1:T(8,128)(2,1)S(1)} %collective-permute-done.23), channel_id=1, source_target_pairs={{0,16},{16,0},{2,18},{18,2},{4,20},{20,4},{6,22},{22,6},{8,24},{24... | collective-permute-start | bytes 393224 | tf_op jit(solution)/shard_map/ppermute | solution.py:17
  642.2 24.1 %collective-permute-start.25 = (bf16[2,2,2,64,128]{4,3,0,2,1:T(8,128)(2,1)S(1)}, bf16[2,2,2,64,128]{4,3,0,2,1:T(8,128)(2,1)S(1)}, u32[]{:S(2)}, u32[]{:S(2)}) collective-permute-start(bf16[2,2,2,64,128]{4,3,0,2,1:T(8,128)(2,1)S(1)} %collective-permute-done.24), channel_id=1, source_target_pairs={{0,32},{32,0},{2,34},{34,2},{4,36},{36,4},{6,38},{38,6},{8,40},{40... | collective-permute-start | bytes 393224 | tf_op jit(solution)/shard_map/ppermute | solution.py:17
  666.3 6.8 collective-permute-start.26
  673.2 8.4 %collective-permute-start.27 = (bf16[2,2,2,64,128]{4,3,0,2,1:T(8,128)(2,1)S(1)}, bf16[2,2,2,64,128]{4,3,0,2,1:T(8,128)(2,1)S(1)}, u32[]{:S(2)}, u32[]{:S(2)}) collective-permute-start(bf16[2,2,2,64,128]{4,3,0,2,1:T(8,128)(2,1)S(1)} %collective-permute-done.26), channel_id=1, source_target_pairs={{0,128},{128,0},{2,130},{130,2},{4,132},{132,4},{6,134},{134,6},{8... | collective-permute-start | bytes 393224 | tf_op jit(solution)/shard_map/ppermute | solution.py:17
  (58 other events, 541.6 us)
Sparse Core Ops, SparseCore 0:
  536.4 57.7 reduce-scatter.3
